TPU v7x, 32 devices: a whole 2x2x4 slice. The times are simulated.
32 devices in a mesh: replica: 4 (over y, core), tensor: 8 (over z, x).
Axes of the slice: x: 2, y: 2, z: 4, core: 2. Of those that a mesh axis runs over, the one named last changes fastest.
Arguments:
- tokens: bfloat16 [4, 2048, 8192], P('replica', None, 'tensor'), may hold values from -6 to 6
- kv_grad: bfloat16 [4, 2048, 1024], P('replica', None, 'tensor'), may hold values from -6 to 6
- weights: float32 [4, 8192, 1024], P('replica', 'tensor'), may hold values from -0.0625 to 0.0625
- first_moment: bfloat16 [4, 8192, 1024], P('replica', 'tensor'), may hold values from -240 to 240
- second_moment: bfloat16 [4, 8192, 1024], P('replica', 'tensor'), may hold values from 300 to 5984
- exponent: int32 [8], replicated, may hold values from 0 to 1, as said below
Outputs:
- new_weights: float32 [4, 8192, 1024], P('replica', 'tensor')
- new_first: bfloat16 [4, 8192, 1024], P('replica', 'tensor')
- new_second: bfloat16 [4, 8192, 1024], P('replica', 'tensor')
- input_grad: bfloat16 [4, 2048, 8192], P('replica', None, 'tensor')
Inputs may be any that keep to these rules, and one draw needn't show every extreme that they name: One integer per column bucket; the gossip partner of bucket g lies 2 ** exponent[g] replicas away; some bucket takes 0 and some bucket takes the largest allowed value.
All inputs are finite; a program needn't handle non-finite values.
Results may differ from a plain program's by a relative error of at most 0.0049.
Values may be sent and summed in bfloat16 or wider, within the bound.
A program may use at most 128 MiB of HBM per device.

v0:
```python
import jax
import jax.numpy as jnp
from jax import lax
from jax.sharding import PartitionSpec as P

learn_rate = 0.00015
beta_first = 0.9
beta_second = 0.95
decay_rate = 0.1
epsilon = 1e-08


def for_sending(array):
    return jax.tree.map(lambda a: a.astype(jnp.bfloat16) if a.dtype == jnp.float32 else a, array)


def from_behind(array, axis, by):
    count = lax.axis_size(axis)
    return lax.ppermute(array, axis, [(i, (i + by) % count) for i in range(count)])


def build_branch(hop_count):

    def fetch_peer(source_array):
        return jax.tree.map(
            lambda part, own: part.astype(own.dtype),
            from_behind(for_sending(source_array), "replica", hop_count),
            source_array,
        )

    return fetch_peer


def bucket_gossip(source_array, exponent, builder):
    levels = lax.axis_size("replica").bit_length() - 1
    branches = [builder(1 << bit_index) for bit_index in range(levels)]
    bucket_count = exponent.shape[0]
    bucket_width = source_array.shape[2] // bucket_count
    pieces = []
    for bucket_index in range(bucket_count):
        columns = source_array[
            :, :, bucket_index * bucket_width : (bucket_index + 1) * bucket_width
        ]
        pieces.append(lax.switch(exponent[bucket_index], branches, columns))
    return jnp.concatenate(pieces, axis=2)


def adam_update(master_part, partner_part, grad_part, first_part, second_part):
    averaged = 0.5 * (master_part + partner_part)
    first = beta_first * first_part.astype(jnp.float32) + (1.0 - beta_first) * grad_part
    second = (
        beta_second * second_part.astype(jnp.float32) + (1.0 - beta_second) * grad_part * grad_part
    )
    direction = first / (jnp.sqrt(second) + epsilon)
    new_weights = averaged - learn_rate * (direction + decay_rate * averaged)
    return (new_weights, first.astype(jnp.bfloat16), second.astype(jnp.bfloat16))


def on_device(tokens, kv_grad, weights, first_moment, second_moment, exponent):
    acts = tokens[0]
    local_cols = kv_grad[0]
    master = weights[0]
    master_low = master.astype(jnp.bfloat16)
    whole_grad = lax.all_gather(local_cols, "tensor", axis=1, tiled=True)
    grad_here = jnp.dot(acts.T, whole_grad, preferred_element_type=jnp.float32)
    back = jnp.dot(whole_grad, master_low.T, preferred_element_type=jnp.float32)
    partner = bucket_gossip(weights, exponent, build_branch)
    new_weights, new_first, new_second = adam_update(
        master, partner[0], grad_here, first_moment[0], second_moment[0]
    )
    return (new_weights[None], new_first[None], new_second[None], back.astype(jnp.bfloat16)[None])


def solution(mesh):
    placed = (
        P("replica", None, "tensor"),
        P("replica", None, "tensor"),
        P("replica", "tensor", None),
        P("replica", "tensor", None),
        P("replica", "tensor", None),
        P(),
    )
    return jax.shard_map(
        on_device,
        mesh=mesh,
        in_specs=placed,
        out_specs=(
            P("replica", "tensor", None),
            P("replica", "tensor", None),
            P("replica", "tensor", None),
            P("replica", None, "tensor"),
        ),
        check_vma=False,
    )
```

profile of v0, /device:TPU:0, one launch (start us, length us, event | category | flops | bytes accessed | tf_op | source)
XLA Modules:
  0.0 116.2 jit_solution(7453863151235359083)
XLA Ops:
  7.2 0.0 all-gather.3.cloned.1.call-start
  7.2 0.7 all-gather.3.cloned.1.call-update
  7.9 1.6 %fusion.18 = (s32[1]{0:T(128)}, s32[1]{0:T(128)}, s32[1]{0:T(128)}, s32[1]{0:T(128)}, s32[1]{0:T(128)}, /*index=5*/s32[1]{0:T(128)}, s32[1]{0:T(128)}, s32[1]{0:T(128)}) fusion(s32[8]{0:T(128)} %param.27), kind=kLoop, calls=%fused_computation.28 | loop fusion | bytes 64 | tf_op jit(solution)/shard_map/slice | solution.py:44
  14.8 3.2 %fusion.17 = (bf16[1,1024,128]{2,1,0:T(8,128)(2,1)S(1)}, bf16[1,1024,128]{2,1,0:T(8,128)(2,1)}, bf16[1,1024,128]{2,1,0:T(8,128)(2,1)S(1)}, bf16[1,1024,128]{2,1,...) fusion(f32[1,1024,1024]{2,1,0:T(8,128)} %param.24), kind=kLoop, calls=%fused_computation.27 | loop fusion | bytes 4194304 | tf_op jit(solution)/shard_map/slice | solution.py:41
  18.0 6.5 %conditional.32 = (f32[1,1024,128]{2,1,0:T(8,128)S(1)}) conditional(s32[]{:T(128)} %bitcast, bf16[1,1024,128]{2,1,0:T(8,128)(2,1)S(1)} %get-tuple-element.102, bf16[1,1024,128]{2,1,0:T(8,128)(2,1)S(1)} %get-tuple-element.102), branch_computations={%region_0.0_spmd, %region_1.0_spmd} | conditional | flops 131072 | bytes 1835056
  18.0 0.5 collective-permute-start
  18.5 6.0 %collective-permute-done = bf16[1,1024,128]{2,1,0:T(8,128)(2,1)S(1)} collective-permute-done((bf16[1,1024,128]{2,1,0:T(8,128)(2,1)S(1)}, bf16[1,1024,128]{2,1,0:T(8,128)(2,1)S(1)}, u32[]{:S(2)}, u32[]{:S(2)}) %collective-permute-start) | collective-permute-done | bytes 262176 | tf_op jit(solution)/shard_map/cond/branch_0_fun/ppermute | solution.py:19
  24.5 5.9 %conditional.33 = (f32[1,1024,128]{2,1,0:T(8,128)S(1)}) conditional(s32[]{:T(128)} %bitcast.1, bf16[1,1024,128]{2,1,0:T(8,128)(2,1)S(1)} %get-tuple-element.101, bf16[1,1024,128]{2,1,0:T(8,128)(2,1)S(1)} %get-tuple-element.101), branch_computations={%region_2.0_spmd, %region_3.0_spmd} | conditional | flops 131072 | bytes 1835056
  24.6 0.1 collective-permute-start.2
  24.6 5.8 %collective-permute-done.2 = bf16[1,1024,128]{2,1,0:T(8,128)(2,1)S(1)} collective-permute-done((bf16[1,1024,128]{2,1,0:T(8,128)(2,1)S(1)}, bf16[1,1024,128]{2,1,0:T(8,128)(2,1)S(1)}, u32[]{:S(2)}, u32[]{:S(2)}) %collective-permute-start.2) | collective-permute-done | bytes 262176 | tf_op jit(solution)/shard_map/cond/branch_0_fun/ppermute | solution.py:19
  30.5 5.9 %conditional.34 = (f32[1,1024,128]{2,1,0:T(8,128)S(1)}) conditional(s32[]{:T(128)} %bitcast.2, bf16[1,1024,128]{2,1,0:T(8,128)(2,1)S(1)} %get-tuple-element.100, bf16[1,1024,128]{2,1,0:T(8,128)(2,1)S(1)} %get-tuple-element.100), branch_computations={%region_4.0_spmd, %region_5.0_spmd} | conditional | flops 131072 | bytes 1835056
  30.5 0.1 collective-permute-start.4
  30.5 5.8 %collective-permute-done.4 = bf16[1,1024,128]{2,1,0:T(8,128)(2,1)S(1)} collective-permute-done((bf16[1,1024,128]{2,1,0:T(8,128)(2,1)S(1)}, bf16[1,1024,128]{2,1,0:T(8,128)(2,1)S(1)}, u32[]{:S(2)}, u32[]{:S(2)}) %collective-permute-start.4) | collective-permute-done | bytes 262176 | tf_op jit(solution)/shard_map/cond/branch_0_fun/ppermute | solution.py:19
  36.4 8.3 %conditional.35 = (f32[1,1024,128]{2,1,0:T(8,128)S(1)}) conditional(s32[]{:T(128)} %bitcast.3, bf16[1,1024,128]{2,1,0:T(8,128)(2,1)S(1)} %get-tuple-element.99, bf16[1,1024,128]{2,1,0:T(8,128)(2,1)S(1)} %get-tuple-element.99), branch_computations={%region_6.0_spmd, %region_7.0_spmd} | conditional | flops 131072 | bytes 1835056
  36.4 2.4 %collective-permute-start.7 = (bf16[1,1024,128]{2,1,0:T(8,128)(2,1)S(1)}, bf16[1,1024,128]{2,1,0:T(8,128)(2,1)S(1)}, u32[]{:S(2)}, u32[]{:S(2)}) collective-permute-start(bf16[1,1024,128]{2,1,0:T(8,128)(2,1)S(1)} %param.7), channel_id=1, source_target_pairs={{0,16},{8,24},{16,0},{24,8},{1,17},{9,25},{17,1},{25,9},{2,18},{10... | collective-permute-start | bytes 786440 | tf_op jit(solution)/shard_map/cond/branch_1_fun/ppermute | solution.py:19
  38.8 5.8 %collective-permute-done.7 = bf16[1,1024,128]{2,1,0:T(8,128)(2,1)S(1)} collective-permute-done((bf16[1,1024,128]{2,1,0:T(8,128)(2,1)S(1)}, bf16[1,1024,128]{2,1,0:T(8,128)(2,1)S(1)}, u32[]{:S(2)}, u32[]{:S(2)}) %collective-permute-start.7) | collective-permute-done | bytes 262176 | tf_op jit(solution)/shard_map/cond/branch_1_fun/ppermute | solution.py:19
  44.6 5.9 %conditional.36 = (f32[1,1024,128]{2,1,0:T(8,128)S(1)}) conditional(s32[]{:T(128)} %bitcast.4, bf16[1,1024,128]{2,1,0:T(8,128)(2,1)S(1)} %get-tuple-element.98, bf16[1,1024,128]{2,1,0:T(8,128)(2,1)S(1)} %get-tuple-element.98), branch_computations={%region_8.0_spmd, %region_9.0_spmd} | conditional | flops 131072 | bytes 1835056
  44.7 0.1 collective-permute-start.8
  44.7 5.8 %collective-permute-done.8 = bf16[1,1024,128]{2,1,0:T(8,128)(2,1)S(1)} collective-permute-done((bf16[1,1024,128]{2,1,0:T(8,128)(2,1)S(1)}, bf16[1,1024,128]{2,1,0:T(8,128)(2,1)S(1)}, u32[]{:S(2)}, u32[]{:S(2)}) %collective-permute-start.8) | collective-permute-done | bytes 262176 | tf_op jit(solution)/shard_map/cond/branch_0_fun/ppermute | solution.py:19
  50.6 6.5 %conditional.37 = (f32[1,1024,128]{2,1,0:T(8,128)S(1)}) conditional(s32[]{:T(128)} %bitcast.5, bf16[1,1024,128]{2,1,0:T(8,128)(2,1)S(1)} %get-tuple-element.97, bf16[1,1024,128]{2,1,0:T(8,128)(2,1)S(1)} %get-tuple-element.97), branch_computations={%region_10.0_spmd, %region_11.0_spmd} | conditional | flops 131072 | bytes 1835056
  50.6 0.6 collective-permute-start.11
  51.2 5.8 %collective-permute-done.11 = bf16[1,1024,128]{2,1,0:T(8,128)(2,1)S(1)} collective-permute-done((bf16[1,1024,128]{2,1,0:T(8,128)(2,1)S(1)}, bf16[1,1024,128]{2,1,0:T(8,128)(2,1)S(1)}, u32[]{:S(2)}, u32[]{:S(2)}) %collective-permute-start.11) | collective-permute-done | bytes 262176 | tf_op jit(solution)/shard_map/cond/branch_1_fun/ppermute | solution.py:19
  57.1 7.5 %conditional.38 = (f32[1,1024,128]{2,1,0:T(8,128)}) conditional(s32[]{:T(128)} %bitcast.6, bf16[1,1024,128]{2,1,0:T(8,128)(2,1)} %get-tuple-element.96, bf16[1,1024,128]{2,1,0:T(8,128)(2,1)} %get-tuple-element.96), branch_computations={%region_12.0_spmd, %region_13.0_spmd} | conditional | flops 131072 | bytes 1835056
  57.1 1.6 %collective-permute-start.13 = (bf16[1,1024,128]{2,1,0:T(8,128)(2,1)}, bf16[1,1024,128]{2,1,0:T(8,128)(2,1)S(1)}, u32[]{:S(2)}, u32[]{:S(2)}) collective-permute-start(bf16[1,1024,128]{2,1,0:T(8,128)(2,1)} %param.13), channel_id=1, source_target_pairs={{0,16},{8,24},{16,0},{24,8},{1,17},{9,25},{17,1},{25,9},{2,18},{10... | collective-permute-start | bytes 786440 | tf_op jit(solution)/shard_map/cond/branch_1_fun/ppermute | solution.py:19
  58.7 5.1 %collective-permute-done.13 = bf16[1,1024,128]{2,1,0:T(8,128)(2,1)S(1)} collective-permute-done((bf16[1,1024,128]{2,1,0:T(8,128)(2,1)}, bf16[1,1024,128]{2,1,0:T(8,128)(2,1)S(1)}, u32[]{:S(2)}, u32[]{:S(2)}) %collective-permute-start.13) | collective-permute-done | bytes 262176 | tf_op jit(solution)/shard_map/cond/branch_1_fun/ppermute | solution.py:19
  63.7 0.8 convert_element_type.155
  64.6 6.6 %conditional.39 = (f32[1,1024,128]{2,1,0:T(8,128)}) conditional(s32[]{:T(128)} %bitcast.7, bf16[1,1024,128]{2,1,0:T(8,128)(2,1)S(1)} %get-tuple-element.95, bf16[1,1024,128]{2,1,0:T(8,128)(2,1)S(1)} %get-tuple-element.95), branch_computations={%region_14.0_spmd, %region_15.0_spmd} | conditional | flops 131072 | bytes 1835056
  64.6 0.0 collective-permute-start.14
  64.6 5.8 %collective-permute-done.14 = bf16[1,1024,128]{2,1,0:T(8,128)(2,1)S(1)} collective-permute-done((bf16[1,1024,128]{2,1,0:T(8,128)(2,1)S(1)}, bf16[1,1024,128]{2,1,0:T(8,128)(2,1)S(1)}, u32[]{:S(2)}, u32[]{:S(2)}) %collective-permute-start.14) | collective-permute-done | bytes 262176 | tf_op jit(solution)/shard_map/cond/branch_0_fun/ppermute | solution.py:19
  70.4 0.8 convert_element_type.157
  71.2 0.8 constant_dynamic-update-slice_fusion.7
  72.0 0.8 constant_dynamic-update-slice_fusion.6
  72.9 0.8 constant_dynamic-update-slice_fusion.5
  73.7 0.8 constant_dynamic-update-slice_fusion.4
  74.5 0.8 constant_dynamic-update-slice_fusion.3
  75.3 0.8 constant_dynamic-update-slice_fusion.2
  76.2 0.0 copy-done
  76.2 0.8 constant_dynamic-update-slice_fusion.1
  77.0 0.0 copy-done.1
  77.0 0.8 constant_dynamic-update-slice_fusion
  77.8 10.0 %all-gather.3.cloned.1.call-done = bf16[1,2048,1024]{2,1,0:T(8,128)(2,1)} async-done(((bf16[1,2048,128]{2,1,0:T(8,128)(2,1)}), bf16[1,2048,1024]{2,1,0:T(8,128)(2,1)}) %all-gather.3.cloned.1.call-update) | async-done | bytes 4194320 | tf_op jit(solution)/shard_map/all_gather | solution.py:64
  87.8 10.2 %convert_bitcast_fusion = bf16[1,2048,1024]{2,1,0:T(8,128)(2,1)} fusion(bf16[1,2048,1024]{2,1,0:T(8,128)(2,1)} %all-gather.3.cloned.1.call-done, f32[1,1024,1024]{2,1,0:T(8,128)} %param.24), kind=kOutput, calls=%fused_computation.12 | convolution fusion | flops 4298113024 | bytes 12582912 | tf_op jit(solution)/shard_map/dot_general | solution.py:66
  98.0 0.0 copy-done.2
  98.0 0.0 copy-done.3
  98.0 0.0 copy-done.4
  98.0 0.0 copy-done.5
  98.0 0.0 copy-done.6
  98.0 11.3 %fusion.13 = (bf16[1,1024,1024]{2,1,0:T(8,128)(2,1)}, f32[1,1024,1024]{2,1,0:T(8,128)}, bf16[1,1024,1024]{2,1,0:T(8,128)(2,1)}) fusion(bf16[1,1024,1024]{2,1,0:T(8,128)(2,1)S(1)} %copy-done.5, bf16[1,1024,1024]{2,1,0:T(8,128)(2,1)S(1)} %copy-done.6, f32[1,1024,1024]{2,1,0:T(8,128)S(1)} %copy-done.2, f32[1,1024,1024]{2,1,0:T(8,128)} %constant_dynamic-update-slice_fusion, ...), kind=kOutput, calls=%fused_computation.15 | convolution fusion | flops 4314890240 | bytes 29360128 | tf_op jit(solution)/shard_map/dot_general | solution.py:65
  (13 shorter events, 0.2 us)
Async XLA Ops:
  7.2 80.6 %all-gather.3.cloned.1.call-start = ((), (), s32[]{:S(2)}) async-start(), calls=%async_computation | async-start | bytes 4718592 | tf_op jit(solution)/shard_map/all_gather | solution.py:64
  18.0 6.5 %collective-permute-start = (bf16[1,1024,128]{2,1,0:T(8,128)(2,1)S(1)}, bf16[1,1024,128]{2,1,0:T(8,128)(2,1)S(1)}, u32[]{:S(2)}, u32[]{:S(2)}) collective-permute-start(bf16[1,1024,128]{2,1,0:T(8,128)(2,1)S(1)} %param), channel_id=1, source_target_pairs={{0,8},{8,16},{16,24},{24,0},{1,9},{9,17},{17,25},{25,1},{2,10},{10... | collective-permute-start | bytes 786440 | tf_op jit(solution)/shard_map/cond/branch_0_fun/ppermute | solution.py:19
  24.6 5.8 %collective-permute-start.2 = (bf16[1,1024,128]{2,1,0:T(8,128)(2,1)S(1)}, bf16[1,1024,128]{2,1,0:T(8,128)(2,1)S(1)}, u32[]{:S(2)}, u32[]{:S(2)}) collective-permute-start(bf16[1,1024,128]{2,1,0:T(8,128)(2,1)S(1)} %param.2), channel_id=1, source_target_pairs={{0,8},{8,16},{16,24},{24,0},{1,9},{9,17},{17,25},{25,1},{2,10},{10... | collective-permute-start | bytes 786440 | tf_op jit(solution)/shard_map/cond/branch_0_fun/ppermute | solution.py:19
  30.5 5.8 %collective-permute-start.4 = (bf16[1,1024,128]{2,1,0:T(8,128)(2,1)S(1)}, bf16[1,1024,128]{2,1,0:T(8,128)(2,1)S(1)}, u32[]{:S(2)}, u32[]{:S(2)}) collective-permute-start(bf16[1,1024,128]{2,1,0:T(8,128)(2,1)S(1)} %param.4), channel_id=1, source_target_pairs={{0,8},{8,16},{16,24},{24,0},{1,9},{9,17},{17,25},{25,1},{2,10},{10... | collective-permute-start | bytes 786440 | tf_op jit(solution)/shard_map/cond/branch_0_fun/ppermute | solution.py:19
  36.4 8.2 %collective-permute-start.7 = (bf16[1,1024,128]{2,1,0:T(8,128)(2,1)S(1)}, bf16[1,1024,128]{2,1,0:T(8,128)(2,1)S(1)}, u32[]{:S(2)}, u32[]{:S(2)}) collective-permute-start(bf16[1,1024,128]{2,1,0:T(8,128)(2,1)S(1)} %param.7), channel_id=1, source_target_pairs={{0,16},{8,24},{16,0},{24,8},{1,17},{9,25},{17,1},{25,9},{2,18},{10... | collective-permute-start | bytes 786440 | tf_op jit(solution)/shard_map/cond/branch_1_fun/ppermute | solution.py:19
  44.7 5.8 %collective-permute-start.8 = (bf16[1,1024,128]{2,1,0:T(8,128)(2,1)S(1)}, bf16[1,1024,128]{2,1,0:T(8,128)(2,1)S(1)}, u32[]{:S(2)}, u32[]{:S(2)}) collective-permute-start(bf16[1,1024,128]{2,1,0:T(8,128)(2,1)S(1)} %param.8), channel_id=1, source_target_pairs={{0,8},{8,16},{16,24},{24,0},{1,9},{9,17},{17,25},{25,1},{2,10},{10... | collective-permute-start | bytes 786440 | tf_op jit(solution)/shard_map/cond/branch_0_fun/ppermute | solution.py:19
  50.6 6.4 %collective-permute-start.11 = (bf16[1,1024,128]{2,1,0:T(8,128)(2,1)S(1)}, bf16[1,1024,128]{2,1,0:T(8,128)(2,1)S(1)}, u32[]{:S(2)}, u32[]{:S(2)}) collective-permute-start(bf16[1,1024,128]{2,1,0:T(8,128)(2,1)S(1)} %param.11), channel_id=1, source_target_pairs={{0,16},{8,24},{16,0},{24,8},{1,17},{9,25},{17,1},{25,9},{2,18},{10... | collective-permute-start | bytes 786440 | tf_op jit(solution)/shard_map/cond/branch_1_fun/ppermute | solution.py:19
  57.1 6.6 %collective-permute-start.13 = (bf16[1,1024,128]{2,1,0:T(8,128)(2,1)}, bf16[1,1024,128]{2,1,0:T(8,128)(2,1)S(1)}, u32[]{:S(2)}, u32[]{:S(2)}) collective-permute-start(bf16[1,1024,128]{2,1,0:T(8,128)(2,1)} %param.13), channel_id=1, source_target_pairs={{0,16},{8,24},{16,0},{24,8},{1,17},{9,25},{17,1},{25,9},{2,18},{10... | collective-permute-start | bytes 786440 | tf_op jit(solution)/shard_map/cond/branch_1_fun/ppermute | solution.py:19
  64.6 5.8 %collective-permute-start.14 = (bf16[1,1024,128]{2,1,0:T(8,128)(2,1)S(1)}, bf16[1,1024,128]{2,1,0:T(8,128)(2,1)S(1)}, u32[]{:S(2)}, u32[]{:S(2)}) collective-permute-start(bf16[1,1024,128]{2,1,0:T(8,128)(2,1)S(1)} %param.14), channel_id=1, source_target_pairs={{0,8},{8,16},{16,24},{24,0},{1,9},{9,17},{17,25},{25,1},{2,10},{10... | collective-permute-start | bytes 786440 | tf_op jit(solution)/shard_map/cond/branch_0_fun/ppermute | solution.py:19
  71.2 5.0 %copy-start = (f32[1,1024,128]{2,1,0:T(8,128)S(1)}, f32[1,1024,128]{2,1,0:T(8,128)}, u32[]{:S(2)}) copy-start(f32[1,1024,128]{2,1,0:T(8,128)} %get-tuple-element.117) | copy-start | bytes 1572868
  71.2 5.8 %copy-start.1 = (f32[1,1024,128]{2,1,0:T(8,128)S(1)}, f32[1,1024,128]{2,1,0:T(8,128)}, u32[]{:S(2)}) copy-start(f32[1,1024,128]{2,1,0:T(8,128)} %get-tuple-element.118) | copy-start | bytes 1572868
  87.8 10.2 %copy-start.2 = (f32[1,1024,1024]{2,1,0:T(8,128)S(1)}, f32[1,1024,1024]{2,1,0:T(8,128)}, u32[]{:S(2)}) copy-start(f32[1,1024,1024]{2,1,0:T(8,128)} %param.24) | copy-start | bytes 12582916
  87.8 10.2 %copy-start.3 = (bf16[1,2048,1024]{2,1,0:T(8,128)(2,1)S(1)}, bf16[1,2048,1024]{2,1,0:T(8,128)(2,1)}, u32[]{:S(2)}) copy-start(bf16[1,2048,1024]{2,1,0:T(8,128)(2,1)} %param.22) | copy-start | bytes 12582916
  87.8 10.2 %copy-start.4 = (bf16[1,2048,1024]{2,1,0:T(8,128)(2,1)S(1)}, bf16[1,2048,1024]{2,1,0:T(8,128)(2,1)}, u32[]{:S(2)}) copy-start(bf16[1,2048,1024]{2,1,0:T(8,128)(2,1)} %all-gather.3.cloned.1.call-done) | copy-start | bytes 12582916
  87.8 10.2 %copy-start.5 = (bf16[1,1024,1024]{2,1,0:T(8,128)(2,1)S(1)}, bf16[1,1024,1024]{2,1,0:T(8,128)(2,1)}, u32[]{:S(2)}) copy-start(bf16[1,1024,1024]{2,1,0:T(8,128)(2,1)} %param.26) | copy-start | bytes 6291460
  87.8 10.2 %copy-start.6 = (bf16[1,1024,1024]{2,1,0:T(8,128)(2,1)S(1)}, bf16[1,1024,1024]{2,1,0:T(8,128)(2,1)}, u32[]{:S(2)}) copy-start(bf16[1,1024,1024]{2,1,0:T(8,128)(2,1)} %param.25) | copy-start | bytes 6291460
Sparse Core Ops, SparseCore 0:
  10.0 77.7 all-gather.2
where the time goes:
time: 116 us
  waiting for transfers between devices  56.6 us (49%)
  matrix products  21.5 us (19%)
  between operations  19.4 us (17%)
  local copies, waits for them, and re-layouts  11.5 us (10%)
  starting transfers between devices  5.19 us (4%)
  other arithmetic  1.87 us (2%)
    ppermute x8, waiting for transfers between devices, from_behind(): lax.ppermute(array, axis, [(i, (i + by) % count) for i in range(count)])  45.9 us
    dot_general x1, matrix products, on_device(): grad_here = jnp.dot(acts.T, whole_grad, preferred_element_type=jnp.float32)  11.3 us
    dot_general x1, matrix products, on_device(): back = jnp.dot(whole_grad, master_low.T, preferred_element_type=jnp.float32)  10.2 us
    all_gather x1, waiting for transfers between devices, on_device(): whole_grad = lax.all_gather(local_cols, 'tensor', axis=1, tiled=True)  9.97 us
    unnamed x21, local copies, waits for them, and re-layouts  5.81 us
    ppermute x8, starting transfers between devices, from_behind(): lax.ppermute(array, axis, [(i, (i + by) % count) for i in range(count)])  5.15 us
    slice x1, local copies, waits for them, and re-layouts, bucket_gossip(): source_array[:, :, bucket_index * bucket_width:(bucket_index + 1) * bucke...  3.25 us
  transfers between devices with their start and end apart: 9, of which 9 were waited for; matrix products, arithmetic and copies ran while one was open for 12% of the time, Pallas kernels for 0%

commit v1 on v0

--- a/solution.py
+++ b/solution.py
@@ -61,7 +61,18 @@
     local_cols = kv_grad[0]
     master = weights[0]
     master_low = master.astype(jnp.bfloat16)
-    whole_grad = lax.all_gather(local_cols, "tensor", axis=1, tiled=True)
+    ways = lax.axis_size("tensor")
+    up = [(d, (d + 1) % ways) for d in range(ways)]
+    down = [(d, (d - 1) % ways) for d in range(ways)]
+    earlier, later = ([local_cols], [local_cols])
+    for _ in range(ways // 2):
+        earlier.append(lax.ppermute(earlier[-1], "tensor", up))
+    for _ in range((ways - 1) // 2):
+        later.append(lax.ppermute(later[-1], "tensor", down))
+    line = jnp.concatenate([*earlier[::-1], *later[1:]], axis=1)
+    whole_grad = jnp.roll(
+        line, (lax.axis_index("tensor") - ways // 2) * local_cols.shape[1], axis=1
+    )
     grad_here = jnp.dot(acts.T, whole_grad, preferred_element_type=jnp.float32)
     back = jnp.dot(whole_grad, master_low.T, preferred_element_type=jnp.float32)
     partner = bucket_gossip(weights, exponent, build_branch)

time: 116 us -> 188 us (1.62)
  local copies, waits for them, and re-layouts: 11.5 us -> 61 us
  waiting for transfers between devices: 56.6 us -> 81.7 us
  starting transfers between devices: 5.19 us -> 20.7 us
  between operations: 19.4 us -> 5.95 us
  matrix products: 21.5 us -> 17.7 us
    unnamed x21 -> x46, local copies, waits for them, and re-layouts: 5.81 us -> 42.2 us
    ppermute x0 -> x7, waiting for transfers between devices: none -> 34.5 us  [the longest x4 28.4 us: on_device(): earlier.append(lax.ppermute(earlier[-1], 'tensor', up))]
    ppermute x0 -> x7, starting transfers between devices: none -> 17.2 us  [the longest x3 11.7 us: on_device(): later.append(lax.ppermute(later[-1], 'tensor', down))]
    another operation x0 -> x8, local copies, waits for them, and re-layouts: none -> 11.7 us
    all_gather x1 -> x0, waiting for transfers between devices: 9.97 us -> none  [on_device(): whole_grad = lax.all_gather(local_cols, 'tensor', axis=1, tiled=True)]
    dot_general x1, matrix products: 10.2 us -> 6.28 us  [on_device(): back = jnp.dot(whole_grad, master_low.T, preferred_element_type=jnp.float32)]
  transfers between devices with their start and end apart: 9 -> 15, of which waited for: 9 -> 11; matrix products, arithmetic and copies ran while one was open for 12% -> 24% of each run, Pallas kernels for 0% -> 0%
where the time goes in v1:
time: 188 us; the launch traced here: 187 us
  waiting for transfers between devices  81.7 us (43%)
  local copies, waits for them, and re-layouts  61 us (32%)
  starting transfers between devices  20.7 us (11%)
  matrix products  17.7 us (9%)
  between operations  5.95 us (3%)
    ppermute x8, waiting for transfers between devices, from_behind(): lax.ppermute(array, axis, [(i, (i + by) % count) for i in range(count)])  47.2 us
    unnamed x46, local copies, waits for them, and re-layouts  42.2 us
    ppermute x4, waiting for transfers between devices, on_device(): earlier.append(lax.ppermute(earlier[-1], 'tensor', up))  28.4 us
    another operation x8, local copies, waits for them, and re-layouts  11.7 us
    ppermute x3, starting transfers between devices, on_device(): later.append(lax.ppermute(later[-1], 'tensor', down))  11.7 us
    dot_general x1, matrix products, on_device(): grad_here = jnp.dot(acts.T, whole_grad, preferred_element_type=jnp.float32)  11.4 us
    dot_general x1, matrix products, on_device(): back = jnp.dot(whole_grad, master_low.T, preferred_element_type=jnp.float32)  6.28 us
    ppermute x3, waiting for transfers between devices, on_device(): later.append(lax.ppermute(later[-1], 'tensor', down))  6.09 us
  transfers between devices with their start and end apart: 15, of which 11 were waited for; matrix products, arithmetic and copies ran while one was open for 24% of the time, Pallas kernels for 0%

profile of v1, /device:TPU:0, one launch (start us, length us, event | category | flops | bytes accessed | tf_op | source)
XLA Modules:
  0.0 187.2 jit_solution(9642823332393618683)
XLA Ops:
  0.6 3.0 %collective-permute-start.16 = (bf16[2048,128]{1,0:T(8,128)(2,1)}, bf16[2048,128]{1,0:T(8,128)(2,1)S(1)}, u32[]{:S(2)}, u32[]{:S(2)}) collective-permute-start(bf16[2048,128]{1,0:T(8,128)(2,1)} %bitcast.70), channel_id=1, source_target_pairs={{0,1},{1,2},{2,3},{3,4},{4,5},{5,6},{6,7},{7,0},{8,9},{9,10},{10,1... | collective-permute-start | bytes 1572872 | tf_op jit(solution)/shard_map/ppermute | solution.py:69
  3.6 15.2 %collective-permute-done.16 = bf16[2048,128]{1,0:T(8,128)(2,1)S(1)} collective-permute-done((bf16[2048,128]{1,0:T(8,128)(2,1)}, bf16[2048,128]{1,0:T(8,128)(2,1)S(1)}, u32[]{:S(2)}, u32[]{:S(2)}) %collective-permute-start.16) | collective-permute-done | bytes 524320 | tf_op jit(solution)/shard_map/ppermute | solution.py:69
  18.8 4.7 %collective-permute-start.20 = (bf16[2048,128]{1,0:T(8,128)(2,1)}, bf16[2048,128]{1,0:T(8,128)(2,1)S(1)}, u32[]{:S(2)}, u32[]{:S(2)}) collective-permute-start(bf16[2048,128]{1,0:T(8,128)(2,1)} %bitcast.71), channel_id=1, source_target_pairs={{0,7},{1,0},{2,1},{3,2},{4,3},{5,4},{6,5},{7,6},{8,15},{9,8},{10,9... | collective-permute-start | bytes 1572872 | tf_op jit(solution)/shard_map/ppermute | solution.py:71
  23.5 1.6 fusion.18
  27.7 13.2 %collective-permute-done.17 = bf16[2048,128]{1,0:T(8,128)(2,1)S(1)} collective-permute-done((bf16[2048,128]{1,0:T(8,128)(2,1)S(1)}, bf16[2048,128]{1,0:T(8,128)(2,1)S(1)}, u32[]{:S(2)}, u32[]{:S(2)}) %collective-permute-start.17) | collective-permute-done | bytes 524320 | tf_op jit(solution)/shard_map/ppermute | solution.py:69
  40.9 2.5 %collective-permute-start.18 = (bf16[2048,128]{1,0:T(8,128)(2,1)S(1)}, bf16[2048,128]{1,0:T(8,128)(2,1)}, u32[]{:S(2)}, u32[]{:S(2)}) collective-permute-start(bf16[2048,128]{1,0:T(8,128)(2,1)S(1)} %collective-permute-done.17), channel_id=1, source_target_pairs={{0,1},{1,2},{2,3},{3,4},{4,5},{5,6},{6,7},{7,0},{8,9},{9,10},{10,1... | collective-permute-start | bytes 1572872 | tf_op jit(solution)/shard_map/ppermute | solution.py:69
  43.4 3.4 %fusion.17 = (bf16[1,1024,128]{2,1,0:T(8,128)(2,1)S(1)}, bf16[1,1024,128]{2,1,0:T(8,128)(2,1)}, bf16[1,1024,128]{2,1,0:T(8,128)(2,1)}, bf16[1,1024,128]{2,1,0:T(...) fusion(f32[1,1024,1024]{2,1,0:T(8,128)} %param.24), kind=kLoop, calls=%fused_computation.45 | loop fusion | bytes 4194304 | tf_op jit(solution)/shard_map/slice | solution.py:41
  46.8 5.9 %conditional.32 = (f32[1,1024,128]{1,2,0:T(8,128)S(1)}) conditional(s32[]{:T(128)} %bitcast, bf16[1,1024,128]{2,1,0:T(8,128)(2,1)S(1)} %get-tuple-element.114, bf16[1,1024,128]{2,1,0:T(8,128)(2,1)S(1)} %get-tuple-element.114), branch_computations={%region_0.1_spmd, %region_1.2_spmd} | conditional | bytes 1835056
  46.8 5.8 %collective-permute-done = bf16[1,1024,128]{2,1,0:T(8,128)(2,1)S(1)} collective-permute-done((bf16[1,1024,128]{2,1,0:T(8,128)(2,1)S(1)}, bf16[1,1024,128]{2,1,0:T(8,128)(2,1)S(1)}, u32[]{:S(2)}, u32[]{:S(2)}) %collective-permute-start) | collective-permute-done | bytes 262176 | tf_op jit(solution)/shard_map/cond/branch_0_fun/ppermute | solution.py:19
  52.7 7.1 %conditional.33 = (f32[1,1024,128]{1,2,0:T(8,128)S(1)}) conditional(s32[]{:T(128)} %bitcast.1, bf16[1,1024,128]{2,1,0:T(8,128)(2,1)S(1)} %get-tuple-element.113, bf16[1,1024,128]{2,1,0:T(8,128)(2,1)S(1)} %get-tuple-element.113), branch_computations={%region_2.3_spmd, %region_3.4_spmd} | conditional | bytes 1835056
  52.8 5.9 %collective-permute-done.2 = bf16[1,1024,128]{2,1,0:T(8,128)(2,1)} collective-permute-done((bf16[1,1024,128]{2,1,0:T(8,128)(2,1)S(1)}, bf16[1,1024,128]{2,1,0:T(8,128)(2,1)}, u32[]{:S(2)}, u32[]{:S(2)}) %collective-permute-start.2) | collective-permute-done | bytes 262176 | tf_op jit(solution)/shard_map/cond/branch_0_fun/ppermute | solution.py:19
  59.8 7.1 %conditional.34 = (f32[1,1024,128]{1,2,0:T(8,128)S(1)}) conditional(s32[]{:T(128)} %bitcast.2, bf16[1,1024,128]{2,1,0:T(8,128)(2,1)S(1)} %get-tuple-element.112, bf16[1,1024,128]{2,1,0:T(8,128)(2,1)S(1)} %get-tuple-element.112), branch_computations={%region_4.5_spmd, %region_5.6_spmd} | conditional | bytes 1835056
  59.9 5.9 %collective-permute-done.4 = bf16[1,1024,128]{2,1,0:T(8,128)(2,1)} collective-permute-done((bf16[1,1024,128]{2,1,0:T(8,128)(2,1)S(1)}, bf16[1,1024,128]{2,1,0:T(8,128)(2,1)}, u32[]{:S(2)}, u32[]{:S(2)}) %collective-permute-start.4) | collective-permute-done | bytes 262176 | tf_op jit(solution)/shard_map/cond/branch_0_fun/ppermute | solution.py:19
  66.9 9.3 %conditional.35 = (f32[1,1024,128]{1,2,0:T(8,128)}) conditional(s32[]{:T(128)} %bitcast.3, bf16[1,1024,128]{2,1,0:T(8,128)(2,1)} %get-tuple-element.111, bf16[1,1024,128]{2,1,0:T(8,128)(2,1)} %get-tuple-element.111), branch_computations={%region_6.7_spmd, %region_7.8_spmd} | conditional | bytes 1835056
  66.9 1.4 collective-permute-start.7
  68.3 6.1 %collective-permute-done.7 = bf16[1,1024,128]{2,1,0:T(8,128)(2,1)} collective-permute-done((bf16[1,1024,128]{2,1,0:T(8,128)(2,1)}, bf16[1,1024,128]{2,1,0:T(8,128)(2,1)}, u32[]{:S(2)}, u32[]{:S(2)}) %collective-permute-start.7) | collective-permute-done | bytes 262176 | tf_op jit(solution)/shard_map/cond/branch_1_fun/ppermute | solution.py:19
  74.3 1.9 %copy.31 = f32[1,1024,128]{1,2,0:T(8,128)} copy(bf16[1,1024,128]{2,1,0:T(8,128)(2,1)} %collective-permute-done.7) | data formatting | bytes 786432 | tf_op jit(solution)/shard_map/conditional.11
  78.8 2.2 %collective-permute-start.21 = (bf16[2048,128]{1,0:T(8,128)(2,1)S(1)}, bf16[2048,128]{1,0:T(8,128)(2,1)}, u32[]{:S(2)}, u32[]{:S(2)}) collective-permute-start(bf16[2048,128]{1,0:T(8,128)(2,1)S(1)} %collective-permute-done.20), channel_id=1, source_target_pairs={{0,7},{1,0},{2,1},{3,2},{4,3},{5,4},{6,5},{7,6},{8,15},{9,8},{10,9... | collective-permute-start | bytes 1572872 | tf_op jit(solution)/shard_map/ppermute | solution.py:71
  81.0 1.9 %constant_dynamic-update-slice_fusion.4 = f32[1,1024,1024]{1,2,0:T(8,128)} fusion(f32[1,1024,1024]{1,2,0:T(8,128)} %constant_dynamic-update-slice_fusion.5, f32[1,1024,128]{1,2,0:T(8,128)} %get-tuple-element.99), kind=kLoop, calls=%fused_computation.23 | loop fusion | bytes 1048576
  82.9 5.5 %copy.18 = f32[1,1024,1024]{1,2,0:T(8,128)} copy(f32[1,1024,1024]{2,1,0:T(8,128)} %param.24) | data formatting | bytes 8388608 | tf_op args[2]
  90.9 2.6 %copy.19 = bf16[1,1024,1024]{1,2,0:T(8,128)(2,1)} copy(bf16[1,1024,1024]{2,1,0:T(8,128)(2,1)S(1)} %copy-done.2) | data formatting | bytes 4194304 | tf_op args[3]
  93.4 2.9 %copy.20 = bf16[1,1024,1024]{1,2,0:T(8,128)(2,1)S(1)} copy(bf16[1,1024,1024]{2,1,0:T(8,128)(2,1)} %param.26) | data formatting | bytes 4194304 | tf_op args[4]
  96.3 8.1 %conditional.36 = (f32[1,1024,128]{1,2,0:T(8,128)}) conditional(s32[]{:T(128)} %bitcast.4, bf16[1,1024,128]{2,1,0:T(8,128)(2,1)} %get-tuple-element.110, bf16[1,1024,128]{2,1,0:T(8,128)(2,1)} %get-tuple-element.110), branch_computations={%region_8.9_spmd, %region_9.10_spmd} | conditional | bytes 1835056
  96.4 6.1 %collective-permute-done.8 = bf16[1,1024,128]{2,1,0:T(8,128)(2,1)} collective-permute-done((bf16[1,1024,128]{2,1,0:T(8,128)(2,1)}, bf16[1,1024,128]{2,1,0:T(8,128)(2,1)}, u32[]{:S(2)}, u32[]{:S(2)}) %collective-permute-start.8) | collective-permute-done | bytes 262176 | tf_op jit(solution)/shard_map/cond/branch_0_fun/ppermute | solution.py:19
  102.5 1.9 %copy.32 = f32[1,1024,128]{1,2,0:T(8,128)} copy(bf16[1,1024,128]{2,1,0:T(8,128)(2,1)} %collective-permute-done.8) | data formatting | bytes 786432 | tf_op jit(solution)/shard_map/conditional.12
  104.4 8.8 %conditional.37 = (f32[1,1024,128]{1,2,0:T(8,128)}) conditional(s32[]{:T(128)} %bitcast.5, bf16[1,1024,128]{2,1,0:T(8,128)(2,1)} %get-tuple-element.109, bf16[1,1024,128]{2,1,0:T(8,128)(2,1)} %get-tuple-element.109), branch_computations={%region_10.11_spmd, %region_11.12_spmd} | conditional | bytes 1835056
  105.1 6.2 %collective-permute-done.11 = bf16[1,1024,128]{2,1,0:T(8,128)(2,1)} collective-permute-done((bf16[1,1024,128]{2,1,0:T(8,128)(2,1)}, bf16[1,1024,128]{2,1,0:T(8,128)(2,1)}, u32[]{:S(2)}, u32[]{:S(2)}) %collective-permute-start.11) | collective-permute-done | bytes 262176 | tf_op jit(solution)/shard_map/cond/branch_1_fun/ppermute | solution.py:19
  111.3 1.9 %copy.35 = f32[1,1024,128]{1,2,0:T(8,128)} copy(bf16[1,1024,128]{2,1,0:T(8,128)(2,1)} %collective-permute-done.11) | data formatting | bytes 786432 | tf_op jit(solution)/shard_map/conditional.13
  113.1 8.6 %conditional.38 = (f32[1,1024,128]{1,2,0:T(8,128)}) conditional(s32[]{:T(128)} %bitcast.6, bf16[1,1024,128]{2,1,0:T(8,128)(2,1)} %get-tuple-element.108, bf16[1,1024,128]{2,1,0:T(8,128)(2,1)} %get-tuple-element.108), branch_computations={%region_12.13_spmd, %region_13.14_spmd} | conditional | bytes 1835056
  113.1 1.3 collective-permute-start.13
  114.4 5.4 %collective-permute-done.13 = bf16[1,1024,128]{2,1,0:T(8,128)(2,1)} collective-permute-done((bf16[1,1024,128]{2,1,0:T(8,128)(2,1)}, bf16[1,1024,128]{2,1,0:T(8,128)(2,1)}, u32[]{:S(2)}, u32[]{:S(2)}) %collective-permute-start.13) | collective-permute-done | bytes 262176 | tf_op jit(solution)/shard_map/cond/branch_1_fun/ppermute | solution.py:19
  119.8 1.9 %copy.37 = f32[1,1024,128]{1,2,0:T(8,128)} copy(bf16[1,1024,128]{2,1,0:T(8,128)(2,1)} %collective-permute-done.13) | data formatting | bytes 786432 | tf_op jit(solution)/shard_map/conditional.14
  121.7 7.8 %conditional.39 = (f32[1,1024,128]{1,2,0:T(8,128)}) conditional(s32[]{:T(128)} %bitcast.7, bf16[1,1024,128]{2,1,0:T(8,128)(2,1)S(1)} %get-tuple-element.107, bf16[1,1024,128]{2,1,0:T(8,128)(2,1)S(1)} %get-tuple-element.107), branch_computations={%region_14.15_spmd, %region_15.16_spmd} | conditional | bytes 1835056
  121.7 5.9 %collective-permute-done.14 = bf16[1,1024,128]{2,1,0:T(8,128)(2,1)} collective-permute-done((bf16[1,1024,128]{2,1,0:T(8,128)(2,1)S(1)}, bf16[1,1024,128]{2,1,0:T(8,128)(2,1)}, u32[]{:S(2)}, u32[]{:S(2)}) %collective-permute-start.14) | collective-permute-done | bytes 262176 | tf_op jit(solution)/shard_map/cond/branch_0_fun/ppermute | solution.py:19
  127.6 1.9 %copy.38 = f32[1,1024,128]{1,2,0:T(8,128)} copy(bf16[1,1024,128]{2,1,0:T(8,128)(2,1)} %collective-permute-done.14) | data formatting | bytes 786432 | tf_op jit(solution)/shard_map/conditional.15
  129.5 2.0 %constant_dynamic-update-slice_fusion.3 = f32[1,1024,1024]{1,2,0:T(8,128)} fusion(f32[1,1024,1024]{1,2,0:T(8,128)} %constant_dynamic-update-slice_fusion.4, f32[1,1024,128]{1,2,0:T(8,128)} %get-tuple-element.100), kind=kLoop, calls=%fused_computation.22 | loop fusion | bytes 1048576
  131.5 1.9 %constant_dynamic-update-slice_fusion.2 = f32[1,1024,1024]{1,2,0:T(8,128)} fusion(f32[1,1024,1024]{1,2,0:T(8,128)} %constant_dynamic-update-slice_fusion.3, f32[1,1024,128]{1,2,0:T(8,128)} %get-tuple-element.101), kind=kLoop, calls=%fused_computation.21 | loop fusion | bytes 1048576
  133.4 1.9 %constant_dynamic-update-slice_fusion.1 = f32[1,1024,1024]{1,2,0:T(8,128)} fusion(f32[1,1024,1024]{1,2,0:T(8,128)} %constant_dynamic-update-slice_fusion.2, f32[1,1024,128]{1,2,0:T(8,128)} %get-tuple-element.102), kind=kLoop, calls=%fused_computation.20 | loop fusion | bytes 1048576
  135.3 1.9 %constant_dynamic-update-slice_fusion = f32[1,1024,1024]{1,2,0:T(8,128)} fusion(f32[1,1024,1024]{1,2,0:T(8,128)} %constant_dynamic-update-slice_fusion.1, f32[1,1024,128]{1,2,0:T(8,128)} %get-tuple-element.103), kind=kLoop, calls=%fused_computation.19 | loop fusion | bytes 1048576 | tf_op jit(solution)/shard_map/concatenate | solution.py:45
  137.3 4.7 %collective-permute-start.22 = (bf16[2048,128]{1,0:T(8,128)(2,1)}, bf16[2048,128]{1,0:T(8,128)(2,1)S(1)}, u32[]{:S(2)}, u32[]{:S(2)}) collective-permute-start(bf16[2048,128]{1,0:T(8,128)(2,1)} %collective-permute-done.21), channel_id=1, source_target_pairs={{0,7},{1,0},{2,1},{3,2},{4,3},{5,4},{6,5},{7,6},{8,15},{9,8},{10,9... | collective-permute-start | bytes 1572872 | tf_op jit(solution)/shard_map/ppermute | solution.py:71
  146.4 6.1 %collective-permute-done.22 = bf16[2048,128]{1,0:T(8,128)(2,1)S(1)} collective-permute-done((bf16[2048,128]{1,0:T(8,128)(2,1)}, bf16[2048,128]{1,0:T(8,128)(2,1)S(1)}, u32[]{:S(2)}, u32[]{:S(2)}) %collective-permute-start.22) | collective-permute-done | bytes 524320 | tf_op jit(solution)/shard_map/ppermute | solution.py:71
  152.7 1.4 constant_dynamic-update-slice_fusion.15
  154.1 1.2 constant_dynamic-update-slice_fusion.14
  157.5 6.3 %convert_bitcast_fusion = bf16[1,2048,1024]{2,1,0:T(8,128)(2,1)} fusion(bf16[2048,2048]{1,0:T(8,128)(2,1)S(1)} %constant_dynamic-update-slice_fusion.8, s32[]{:T(128)S(6)} %select_n.14, f32[1,1024,1024]{2,1,0:T(8,128)S(1)} %copy-done), kind=kOutput, calls=%fused_computation.10 | convolution fusion | flops 4298113024 | bytes 12582916 | tf_op jit(solution)/shard_map/dot_general | solution.py:77
  163.8 11.4 %fusion.11 = (bf16[1,1024,1024]{1,2,0:T(8,128)(2,1)}, f32[1,1024,1024]{1,2,0:T(8,128)}, bf16[1,1024,1024]{1,2,0:T(8,128)(2,1)}) fusion(bf16[1,1024,1024]{1,2,0:T(8,128)(2,1)S(1)} %copy.20, bf16[1,1024,1024]{1,2,0:T(8,128)(2,1)S(1)} %copy-done.3, f32[1,1024,1024]{1,2,0:T(8,128)S(1)} %copy-done.1, f32[1,1024,1024]{1,2,0:T(8,128)} %constant_dynamic-update-slice_fusion, ...), kind=kOutput, calls=%fused_computation.15 | convolution fusion | flops 4314890240 | bytes 29360132 | tf_op jit(solution)/shard_map/dot_general | solution.py:76
  175.2 5.3 %copy.21 = f32[1,1024,1024]{2,1,0:T(8,128)} copy(f32[1,1024,1024]{1,2,0:T(8,128)} %get-tuple-element.105) | data formatting | bytes 8388608
  180.6 4.1 %copy.22 = bf16[1,1024,1024]{2,1,0:T(8,128)(2,1)} copy(bf16[1,1024,1024]{1,2,0:T(8,128)(2,1)} %get-tuple-element.106) | data formatting | bytes 4194304
  184.7 2.5 %copy.23 = bf16[1,1024,1024]{2,1,0:T(8,128)(2,1)} copy(bf16[1,1024,1024]{1,2,0:T(8,128)(2,1)S(1)} %copy-done.4) | data formatting | bytes 4194304
  (50 shorter events, 12.4 us)
Async XLA Ops:
  0.6 18.2 %collective-permute-start.16 = (bf16[2048,128]{1,0:T(8,128)(2,1)}, bf16[2048,128]{1,0:T(8,128)(2,1)S(1)}, u32[]{:S(2)}, u32[]{:S(2)}) collective-permute-start(bf16[2048,128]{1,0:T(8,128)(2,1)} %bitcast.70), channel_id=1, source_target_pairs={{0,1},{1,2},{2,3},{3,4},{4,5},{5,6},{6,7},{7,0},{8,9},{9,10},{10,1... | collective-permute-start | bytes 1572872 | tf_op jit(solution)/shard_map/ppermute | solution.py:69
  18.8 22.1 %collective-permute-start.17 = (bf16[2048,128]{1,0:T(8,128)(2,1)S(1)}, bf16[2048,128]{1,0:T(8,128)(2,1)S(1)}, u32[]{:S(2)}, u32[]{:S(2)}) collective-permute-start(bf16[2048,128]{1,0:T(8,128)(2,1)S(1)} %collective-permute-done.16), channel_id=1, source_target_pairs={{0,1},{1,2},{2,3},{3,4},{4,5},{5,6},{6,7},{7,0},{8,9},{9,10},{10,1... | collective-permute-start | bytes 1572872 | tf_op jit(solution)/shard_map/ppermute | solution.py:69
  18.8 60.0 %collective-permute-start.20 = (bf16[2048,128]{1,0:T(8,128)(2,1)}, bf16[2048,128]{1,0:T(8,128)(2,1)S(1)}, u32[]{:S(2)}, u32[]{:S(2)}) collective-permute-start(bf16[2048,128]{1,0:T(8,128)(2,1)} %bitcast.71), channel_id=1, source_target_pairs={{0,7},{1,0},{2,1},{3,2},{4,3},{5,4},{6,5},{7,6},{8,15},{9,8},{10,9... | collective-permute-start | bytes 1572872 | tf_op jit(solution)/shard_map/ppermute | solution.py:71
  40.9 18.9 %copy-start.6 = (bf16[2048,128]{1,0:T(8,128)(2,1)}, bf16[2048,128]{1,0:T(8,128)(2,1)S(1)}, u32[]{:S(2)}) copy-start(bf16[2048,128]{1,0:T(8,128)(2,1)S(1)} %collective-permute-done.17) | copy-start | bytes 1572868
  40.9 40.1 %collective-permute-start.18 = (bf16[2048,128]{1,0:T(8,128)(2,1)S(1)}, bf16[2048,128]{1,0:T(8,128)(2,1)}, u32[]{:S(2)}, u32[]{:S(2)}) collective-permute-start(bf16[2048,128]{1,0:T(8,128)(2,1)S(1)} %collective-permute-done.17), channel_id=1, source_target_pairs={{0,1},{1,2},{2,3},{3,4},{4,5},{5,6},{6,7},{7,0},{8,9},{9,10},{10,1... | collective-permute-start | bytes 1572872 | tf_op jit(solution)/shard_map/ppermute | solution.py:69
  46.8 5.8 %collective-permute-start = (bf16[1,1024,128]{2,1,0:T(8,128)(2,1)S(1)}, bf16[1,1024,128]{2,1,0:T(8,128)(2,1)S(1)}, u32[]{:S(2)}, u32[]{:S(2)}) collective-permute-start(bf16[1,1024,128]{2,1,0:T(8,128)(2,1)S(1)} %param), channel_id=1, source_target_pairs={{0,8},{8,16},{16,24},{24,0},{1,9},{9,17},{17,25},{25,1},{2,10},{10... | collective-permute-start | bytes 786440 | tf_op jit(solution)/shard_map/cond/branch_0_fun/ppermute | solution.py:19
  52.8 6.0 %collective-permute-start.2 = (bf16[1,1024,128]{2,1,0:T(8,128)(2,1)S(1)}, bf16[1,1024,128]{2,1,0:T(8,128)(2,1)}, u32[]{:S(2)}, u32[]{:S(2)}) collective-permute-start(bf16[1,1024,128]{2,1,0:T(8,128)(2,1)S(1)} %param.2), channel_id=1, source_target_pairs={{0,8},{8,16},{16,24},{24,0},{1,9},{9,17},{17,25},{25,1},{2,10},{10... | collective-permute-start | bytes 786440 | tf_op jit(solution)/shard_map/cond/branch_0_fun/ppermute | solution.py:19
  59.8 6.0 %collective-permute-start.4 = (bf16[1,1024,128]{2,1,0:T(8,128)(2,1)S(1)}, bf16[1,1024,128]{2,1,0:T(8,128)(2,1)}, u32[]{:S(2)}, u32[]{:S(2)}) collective-permute-start(bf16[1,1024,128]{2,1,0:T(8,128)(2,1)S(1)} %param.4), channel_id=1, source_target_pairs={{0,8},{8,16},{16,24},{24,0},{1,9},{9,17},{17,25},{25,1},{2,10},{10... | collective-permute-start | bytes 786440 | tf_op jit(solution)/shard_map/cond/branch_0_fun/ppermute | solution.py:19
  66.9 7.4 %collective-permute-start.7 = (bf16[1,1024,128]{2,1,0:T(8,128)(2,1)}, bf16[1,1024,128]{2,1,0:T(8,128)(2,1)}, u32[]{:S(2)}, u32[]{:S(2)}) collective-permute-start(bf16[1,1024,128]{2,1,0:T(8,128)(2,1)} %param.7), channel_id=1, source_target_pairs={{0,16},{8,24},{16,0},{24,8},{1,17},{9,25},{17,1},{25,9},{2,18},{10... | collective-permute-start | bytes 786440 | tf_op jit(solution)/shard_map/cond/branch_1_fun/ppermute | solution.py:19
  78.8 58.5 %collective-permute-start.21 = (bf16[2048,128]{1,0:T(8,128)(2,1)S(1)}, bf16[2048,128]{1,0:T(8,128)(2,1)}, u32[]{:S(2)}, u32[]{:S(2)}) collective-permute-start(bf16[2048,128]{1,0:T(8,128)(2,1)S(1)} %collective-permute-done.20), channel_id=1, source_target_pairs={{0,7},{1,0},{2,1},{3,2},{4,3},{5,4},{6,5},{7,6},{8,15},{9,8},{10,9... | collective-permute-start | bytes 1572872 | tf_op jit(solution)/shard_map/ppermute | solution.py:71
  81.0 61.0 %collective-permute-start.19 = (bf16[2048,128]{1,0:T(8,128)(2,1)}, bf16[2048,128]{1,0:T(8,128)(2,1)}, u32[]{:S(2)}, u32[]{:S(2)}) collective-permute-start(bf16[2048,128]{1,0:T(8,128)(2,1)} %collective-permute-done.18), channel_id=1, source_target_pairs={{0,1},{1,2},{2,3},{3,4},{4,5},{5,6},{6,7},{7,0},{8,9},{9,10},{10,1... | collective-permute-start | bytes 1572872 | tf_op jit(solution)/shard_map/ppermute | solution.py:69
  82.9 7.9 %copy-start.2 = (bf16[1,1024,1024]{2,1,0:T(8,128)(2,1)S(1)}, bf16[1,1024,1024]{2,1,0:T(8,128)(2,1)}, u32[]{:S(2)}) copy-start(bf16[1,1024,1024]{2,1,0:T(8,128)(2,1)} %param.25) | copy-start | bytes 6291460
  96.3 6.2 %collective-permute-start.8 = (bf16[1,1024,128]{2,1,0:T(8,128)(2,1)}, bf16[1,1024,128]{2,1,0:T(8,128)(2,1)}, u32[]{:S(2)}, u32[]{:S(2)}) collective-permute-start(bf16[1,1024,128]{2,1,0:T(8,128)(2,1)} %param.8), channel_id=1, source_target_pairs={{0,8},{8,16},{16,24},{24,0},{1,9},{9,17},{17,25},{25,1},{2,10},{10... | collective-permute-start | bytes 786440 | tf_op jit(solution)/shard_map/cond/branch_0_fun/ppermute | solution.py:19
  104.4 6.9 %collective-permute-start.11 = (bf16[1,1024,128]{2,1,0:T(8,128)(2,1)}, bf16[1,1024,128]{2,1,0:T(8,128)(2,1)}, u32[]{:S(2)}, u32[]{:S(2)}) collective-permute-start(bf16[1,1024,128]{2,1,0:T(8,128)(2,1)} %param.11), channel_id=1, source_target_pairs={{0,16},{8,24},{16,0},{24,8},{1,17},{9,25},{17,1},{25,9},{2,18},{10... | collective-permute-start | bytes 786440 | tf_op jit(solution)/shard_map/cond/branch_1_fun/ppermute | solution.py:19
  113.1 6.7 %collective-permute-start.13 = (bf16[1,1024,128]{2,1,0:T(8,128)(2,1)}, bf16[1,1024,128]{2,1,0:T(8,128)(2,1)}, u32[]{:S(2)}, u32[]{:S(2)}) collective-permute-start(bf16[1,1024,128]{2,1,0:T(8,128)(2,1)} %param.13), channel_id=1, source_target_pairs={{0,16},{8,24},{16,0},{24,8},{1,17},{9,25},{17,1},{25,9},{2,18},{10... | collective-permute-start | bytes 786440 | tf_op jit(solution)/shard_map/cond/branch_1_fun/ppermute | solution.py:19
  121.7 5.9 %collective-permute-start.14 = (bf16[1,1024,128]{2,1,0:T(8,128)(2,1)S(1)}, bf16[1,1024,128]{2,1,0:T(8,128)(2,1)}, u32[]{:S(2)}, u32[]{:S(2)}) collective-permute-start(bf16[1,1024,128]{2,1,0:T(8,128)(2,1)S(1)} %param.14), channel_id=1, source_target_pairs={{0,8},{8,16},{16,24},{24,0},{1,9},{9,17},{17,25},{25,1},{2,10},{10... | collective-permute-start | bytes 786440 | tf_op jit(solution)/shard_map/cond/branch_0_fun/ppermute | solution.py:19
  129.5 14.9 %copy-start.7 = (bf16[2048,128]{1,0:T(8,128)(2,1)S(1)}, bf16[2048,128]{1,0:T(8,128)(2,1)}, u32[]{:S(2)}) copy-start(bf16[2048,128]{1,0:T(8,128)(2,1)} %copy-done.6) | copy-start | bytes 1572868
  129.5 15.3 %copy-start.5 = (bf16[1,2048,128]{2,1,0:T(8,128)(2,1)S(1)}, bf16[1,2048,128]{2,1,0:T(8,128)(2,1)}, u32[]{:S(2)}) copy-start(bf16[1,2048,128]{2,1,0:T(8,128)(2,1)} %param.23) | copy-start | bytes 1572868
  137.3 15.2 %collective-permute-start.22 = (bf16[2048,128]{1,0:T(8,128)(2,1)}, bf16[2048,128]{1,0:T(8,128)(2,1)S(1)}, u32[]{:S(2)}, u32[]{:S(2)}) collective-permute-start(bf16[2048,128]{1,0:T(8,128)(2,1)} %collective-permute-done.21), channel_id=1, source_target_pairs={{0,7},{1,0},{2,1},{3,2},{4,3},{5,4},{6,5},{7,6},{8,15},{9,8},{10,9... | collective-permute-start | bytes 1572872 | tf_op jit(solution)/shard_map/ppermute | solution.py:71
  152.7 4.8 %copy-start = (f32[1,1024,1024]{2,1,0:T(8,128)S(1)}, f32[1,1024,1024]{2,1,0:T(8,128)}, u32[]{:S(2)}) copy-start(f32[1,1024,1024]{2,1,0:T(8,128)} %param.24) | copy-start | bytes 12582916
  157.5 6.3 %copy-start.1 = (f32[1,1024,1024]{1,2,0:T(8,128)S(1)}, f32[1,1024,1024]{1,2,0:T(8,128)}, u32[]{:S(2)}) copy-start(f32[1,1024,1024]{1,2,0:T(8,128)} %copy.18) | copy-start | bytes 12582916
  157.5 6.3 %copy-start.3 = (bf16[1,1024,1024]{1,2,0:T(8,128)(2,1)S(1)}, bf16[1,1024,1024]{1,2,0:T(8,128)(2,1)}, u32[]{:S(2)}) copy-start(bf16[1,1024,1024]{1,2,0:T(8,128)(2,1)} %copy.19) | copy-start | bytes 6291460
  157.5 6.3 %copy-start.8 = (bf16[1,2048,1024]{2,1,0:T(8,128)(2,1)S(1)}, bf16[1,2048,1024]{2,1,0:T(8,128)(2,1)}, u32[]{:S(2)}) copy-start(bf16[1,2048,1024]{2,1,0:T(8,128)(2,1)} %param.22) | copy-start | bytes 12582916
  180.6 4.1 %copy-start.4 = (bf16[1,1024,1024]{1,2,0:T(8,128)(2,1)S(1)}, bf16[1,1024,1024]{1,2,0:T(8,128)(2,1)}, u32[]{:S(2)}) copy-start(bf16[1,1024,1024]{1,2,0:T(8,128)(2,1)} %get-tuple-element.104) | copy-start | bytes 6291460
